TPU v7x, 128 devices: a whole 4x4x4 slice. The times are simulated.
128 devices in a mesh: pipe: 16 (over y, x_hi, core), tensor: 8 (over z, x_lo).
Axes of the slice: x: 4 (x_hi: 2, x_lo: 2; x = x_hi * 2 + x_lo), y: 4, z: 4, core: 2. Of those that a mesh axis runs over, the one named last changes fastest.
Arguments:
- forward_input: bfloat16 [16, 512, 4096], P('pipe'), may hold values from -6 to 6
- saved_input: bfloat16 [16, 512, 4096], P('pipe'), may hold values from -6 to 6
- gradient_input: bfloat16 [16, 512, 4096], P('pipe'), may hold values from -6 to 6
- roster: int32 [16, 2], P('pipe'), may hold values from 0 to 1
- sign_bits: int32 [4096], replicated, may hold values from 0 to 1
- gain: float32 [16, 2, 4096], P('pipe'), may hold values from 0.5 to 1.5
- w_query: bfloat16 [16, 2, 4096, 4096], P('pipe', None, None, 'tensor'), may hold values from -0.09375 to 0.09375
- w_key: bfloat16 [16, 2, 4096, 1024], P('pipe', None, None, 'tensor'), may hold values from -0.09375 to 0.09375
- w_value: bfloat16 [16, 2, 4096, 1024], P('pipe', None, None, 'tensor'), may hold values from -0.09375 to 0.09375
- w_out: bfloat16 [16, 2, 4096, 4096], P('pipe', None, 'tensor'), may hold values from -0.09375 to 0.09375
Outputs:
- next_activation: bfloat16 [16, 512, 4096], P('pipe')
- next_gradient: bfloat16 [16, 512, 4096], P('pipe')
All inputs are finite; a program needn't handle non-finite values.
Results may differ from a plain program's by a relative error of at most 0.015.
Values may be sent and summed in bfloat16 or wider, within the bound.
A program may use at most 192 MiB of HBM per device.

v0:
```python
import math
import jax
import jax.numpy as jnp
from jax import lax
from jax.sharding import PartitionSpec as P

HD = 128
HB = 128
eps = 1e-05


def shifted(value, axis, steps):
    count = lax.axis_size(axis)
    pairs = [(source, (source + steps) % count) for source in range(count)]
    return lax.ppermute(value, axis, pairs)


def hadamard(order):
    index = jnp.arange(order, dtype=jnp.int32)
    common = index[:, None] & index[None, :]
    parity = jnp.zeros((order, order), jnp.int32)
    for place in range(order.bit_length() - 1):
        parity = parity ^ common >> place & 1
    return (1 - 2 * parity).astype(jnp.float32)


def rotate(values, signs):
    count = values.shape[0]
    blocks = (values * signs).reshape(count, -1, HB)
    turned = jnp.einsum("rbk,kj->rbj", blocks, hadamard(HB), precision=lax.Precision.HIGHEST)
    return (turned / math.sqrt(HB)).reshape(count, -1)


def unrotate(values, signs):
    count = values.shape[0]
    blocks = values.astype(jnp.float32).reshape(count, -1, HB)
    turned = jnp.einsum("rbk,kj->rbj", blocks, hadamard(HB), precision=lax.Precision.HIGHEST)
    return (turned / math.sqrt(HB)).reshape(count, -1) * signs


def heads_part(inputs, gains, query_w, key_w, value_w, out_w):
    rows = inputs.shape[0]
    kv_count = key_w.shape[1] // HD
    q_count = query_w.shape[1] // HD
    group = q_count // kv_count
    scale = lax.rsqrt(jnp.mean(inputs * inputs, axis=-1, keepdims=True) + eps)
    normed = (inputs * scale * gains).astype(jnp.bfloat16)
    query = jnp.dot(normed, query_w, preferred_element_type=jnp.float32).astype(jnp.bfloat16)
    keys = jnp.dot(normed, key_w, preferred_element_type=jnp.float32).astype(jnp.bfloat16)
    values = jnp.dot(normed, value_w, preferred_element_type=jnp.float32).astype(jnp.bfloat16)
    query = query.reshape(rows, kv_count, group, HD).astype(jnp.float32)
    keys = keys.reshape(rows, kv_count, HD).astype(jnp.float32)
    values = values.reshape(rows, kv_count, HD).astype(jnp.float32)
    scores = jnp.einsum("qkgd,skd->kgqs", query, keys) / math.sqrt(HD)
    position = jnp.arange(rows, dtype=jnp.int32)
    allowed = position[:, None] >= position[None, :]
    scores = jnp.where(allowed, scores, -1e30)
    top = jnp.max(scores, axis=-1, keepdims=True)
    expo = jnp.exp(scores - top)
    probs = (expo / jnp.sum(expo, axis=-1, keepdims=True)).astype(jnp.bfloat16)
    context = jnp.einsum("kgqs,skd->qkgd", probs.astype(jnp.float32), values).astype(jnp.bfloat16)
    context = context.reshape(rows, q_count * HD)
    return jnp.dot(context, out_w, preferred_element_type=jnp.float32)


def pick(stack, which):
    return lax.dynamic_index_in_dim(stack[0], which, 0, keepdims=False)


def local(
    forward_input,
    saved_input,
    gradient_input,
    roster,
    sign_bits,
    gain,
    w_query,
    w_key,
    w_value,
    w_out,
):
    signs = (2 * sign_bits - 1).astype(jnp.float32)
    front = roster[0, 0]
    back = roster[0, 1]
    front_w = (pick(w_query, front), pick(w_key, front), pick(w_value, front), pick(w_out, front))
    back_w = (pick(w_query, back), pick(w_key, back), pick(w_value, back), pick(w_out, back))
    gain_front = pick(gain, front)
    gain_back = pick(gain, back)
    inputs = unrotate(forward_input[0], signs)
    grad = unrotate(gradient_input[0], signs)
    stored = saved_input[0].astype(jnp.float32)
    partial_out = heads_part(inputs, gain_front, *front_w)
    _, pull = jax.vjp(lambda v: heads_part(v, gain_back, *back_w), stored)
    partial_back = pull(grad)[0]
    mixed = lax.psum(partial_out.astype(jnp.bfloat16), "tensor").astype(jnp.float32)
    sent_activation = rotate(inputs + mixed, signs).astype(jnp.bfloat16)
    arrived = shifted(sent_activation, "pipe", 1)
    pulled = lax.psum(partial_back.astype(jnp.bfloat16), "tensor").astype(jnp.float32)
    sent_gradient = rotate(grad + pulled, signs).astype(jnp.bfloat16)
    returned = shifted(sent_gradient, "pipe", -1)
    return (arrived[None], returned[None])


def solution(mesh):
    placed = (
        P("pipe", None, None),
        P("pipe", None, None),
        P("pipe", None, None),
        P("pipe", None),
        P(),
        P("pipe", None, None),
        P("pipe", None, None, "tensor"),
        P("pipe", None, None, "tensor"),
        P("pipe", None, None, "tensor"),
        P("pipe", None, "tensor", None),
    )
    return jax.shard_map(
        local,
        mesh=mesh,
        in_specs=placed,
        out_specs=(P("pipe", None, None), P("pipe", None, None)),
        check_vma=False,
    )
```

profile of v0, /device:TPU:1, one launch (start us, length us, event | category | flops | bytes accessed | tf_op | source)
XLA Modules:
  0.0 628.2 jit_solution(7239126787473838234)
XLA Ops:
  7.2 0.0 copy-start
  7.2 0.0 copy-start.9
  7.2 0.0 all-reduce.3.cloned.1.call-start
  7.2 1.4 fusion.195
  11.2 0.1 iota_compare_fusion
  11.3 3.1 fusion.3
  15.7 0.0 copy-done.10
  15.8 0.0 copy-start.4
  15.8 3.6 fusion.96
  19.5 0.0 copy-start.5
  19.5 4.9 fusion.71
  24.4 0.0 copy-done.5
  24.4 0.0 copy-start.6
  24.4 1.3 copy.33
  25.7 0.9 copy-done.6
  26.6 1.2 copy.34
  27.9 0.0 slice-start.2
  27.9 7.8 %multiply_reduce_fusion = (f32[512]{0:T(512)S(1)}, f32[128,512,32]{1,0,2:T(8,128)S(1)}) fusion(f32[32,128]{1,0:T(8,128)S(1)} %multiply_bitcast_fusion.2, bf16[512,32,128]{2,1,0:T(8,128)(2,1)S(1)} %bitcast.297), kind=kOutput, calls=%fused_computation.27 | convolution fusion | flops 3227909632 | bytes 12601344 | tf_op jit(solution)/shard_map/rbk,kj->rbj/dot_general | solution.py:37
  35.7 0.0 slice-start.3
  35.7 4.2 bitcast_multiply_fusion.3
  39.9 0.0 slice-done.3
  39.9 3.2 fusion.65
  43.2 0.9 fusion.51
  44.0 0.0 copy-start.2
  44.0 2.0 copy-done.2
  46.0 0.9 fusion.118
  47.0 0.0 slice-start.1
  47.0 10.1 %bitcast_multiply_fusion = (bf16[512,32,128]{0,2,1:T(8,128)(2,1)S(1)}, f32[128,512,32]{1,0,2:T(8,128)}) fusion(f32[32,128]{1,0:T(8,128)S(1)} %multiply_bitcast_fusion.2, bf16[512,32,128]{2,1,0:T(8,128)(2,1)S(1)} %bitcast.294), kind=kOutput, calls=%fused_computation.17 | convolution fusion | flops 3225812992 | bytes 16793600 | tf_op jit(solution)/shard_map/rbk,kj->rbj/dot_general | solution.py:37
  57.1 0.0 slice-done
  57.1 0.0 slice-done.1
  57.2 3.1 fusion.68
  60.3 6.9 %convolution_convert_fusion.4 = bf16[4,512,512]{1,2,0:T(8,128)(2,1)} fusion(bf16[128,4,512]{2,0,1:T(8,128)(2,1)} %bitcast.317, bf16[1,2,4096,128]{3,2,1,0:T(8,128)(2,1)} %param.18, s32[]{:T(128)S(6)} %select_n.32, bf16[1,512,4096]{2,1,0:T(8,128)(2,1)} %param.11, f32[4096]{0:T(1024)S(1)} %bitcast.309, f32[512]{0:T(512)S(1)} %fusion.149), kind=kOutput, calls=%fused_computation.89 | convolution fusion | flops 814809088 | bytes 7882756 | tf_op jit(solution)/shard_map/transpose(jvp(kgqs,skd->qkgd))/dot_general | solution.py:61
  67.2 8.8 %convert_reduce_fusion = (f32[4,512]{1,0:T(4,128)S(1)}, pred[1,4,512,512]{2,3,1,0:T(32,128)(4,1)}, f32[4,512]{1,0:T(4,128)S(1)}, f32[4,512]{1,0:T(4,128)S(1)}, f32[512,512,4]{1,0,2:T(8,128)}) fusion(f32[4,512]{1,0:T(4,128)S(1)} %get-tuple-element.20, f32[512,512,4]{1,0,2:T(8,128)} %copy-done.2, pred[512,512]{0,1:T(8,128)(4,1)S(1)} %iota_compare_fusion, ...), kind=kOutput, calls=%fused_computation.62 | convolution fusion | flops 818997248 | bytes 17604612 | tf_op jit(solution)/shard_map/qkgd,skd->kgqs/dot_general | solution.py:54
  76.0 0.0 copy-start.3
  76.0 0.0 copy-start.8
  76.0 0.0 copy-start.14
  76.0 5.4 fusion.189
  81.4 0.5 copy-done.8
  81.9 0.2 copy-done.14
  82.1 3.5 fusion.74
  85.6 9.2 %convolution_convert_fusion = bf16[512,4096]{1,0:T(8,128)(2,1)} fusion(bf16[512,4,128]{0,2,1:T(8,128)(2,1)S(1)} %bitcast.306, pred[1,4,512,512]{2,3,1,0:T(32,128)(4,1)} %get-tuple-element.9, f32[4,512]{1,0:T(4,128)S(1)} %negate_divide_fusion, pred[512,512]{0,1:T(8,128)(4,1)S(1)} %iota_compare_fusion, bf16[1,2,4096,128]{3,2,1,0:T(8,128)(2,1)S(1)} %copy-done, ...), kind=kOutput, calls=%fused_computation.28 | convolution fusion | flops 819003392 | bytes 13402116 | tf_op jit(solution)/shard_map/transpose(jvp())/dot_general | solution.py:49
  94.8 5.8 fusion.77
  100.7 0.0 copy-start.13
  100.7 6.6 %convolution_convert_fusion.3 = bf16[512,4096]{1,0:T(8,128)(2,1)} fusion(bf16[512,512]{0,1:T(8,128)(2,1)S(1)} %bitcast.321, bf16[1,2,512,4096]{3,2,1,0:T(8,128)(2,1)} %param.19, s32[]{:T(128)S(6)} %select_n.30), kind=kOutput, calls=%fused_computation.31 | convolution fusion | flops 2149580800 | bytes 8912900 | tf_op jit(solution)/shard_map/dot_general | solution.py:63
  107.3 0.0 copy-done.13
  107.3 6.8 %convolution_convert_fusion.2 = bf16[512,4096]{1,0:T(8,128)(2,1)} fusion(bf16[512,512]{0,1:T(8,128)(2,1)S(1)} %bitcast.320, bf16[1,2,4096,512]{3,2,1,0:T(8,128)(2,1)} %param.16, s32[]{:T(128)S(6)} %select_n.32), kind=kOutput, calls=%fused_computation.30 | convolution fusion | flops 2149580800 | bytes 8912900 | tf_op jit(solution)/shard_map/transpose(jvp())/dot_general | solution.py:48
  114.1 11.8 %fusion.4 = (f32[512]{0:T(512)S(1)}, bf16[512,4096]{1,0:T(8,128)(2,1)}) fusion(bf16[1,512,4096]{2,1,0:T(8,128)(2,1)} %param.11, f32[4096]{0:T(1024)S(1)} %bitcast.310, bf16[512,4096]{1,0:T(8,128)(2,1)} %convolution_convert_fusion.2, bf16[512,4096]{1,0:T(8,128)(2,1)} %convolution_convert_fusion, bf16[1,2,4096,128]{3,2,1,0:T(8,128)(2,1)S(1)} %copy-done.11, ...), kind=kOutput, calls=%fused_computation.7 | convolution fusion | flops 835780096 | bytes 22841348 | tf_op jit(solution)/shard_map/transpose(jvp())/dot_general | solution.py:50
  125.9 6.1 fusion.7
  132.0 0.0 all-reduce.3.cloned.1.call-update
  132.0 9.0 %copy.13 = f32[512,4096]{1,0:T(8,128)} copy(f32[512,4096]{0,1:T(8,128)} %bitcast.292) | data formatting | bytes 16777216 | tf_op jit(solution)/shard_map/reshape | solution.py:38
  141.0 8.3 %bitcast_multiply_fusion.1 = f32[512,32,128]{0,2,1:T(8,128)} fusion(f32[128,512,32]{1,0,2:T(8,128)} %get-tuple-element.25), kind=kLoop, calls=%fused_computation.18 | loop fusion | flops 2097152 | bytes 16777216 | tf_op jit(solution)/shard_map/div | solution.py:38
  149.3 9.0 %copy.19 = f32[512,4096]{1,0:T(8,128)} copy(f32[512,4096]{0,1:T(8,128)} %bitcast.293) | data formatting | bytes 16777216 | tf_op jit(solution)/shard_map/reshape | solution.py:38
  158.2 317.3 %all-reduce.3.cloned.1.call-done = (bf16[512,4096]{1,0:T(8,128)(2,1)}, bf16[512,4096]{1,0:T(8,128)(2,1)}) async-done(((bf16[512,4096]{1,0:T(8,128)(2,1)}, bf16[512,4096]{1,0:T(8,128)(2,1)}), (bf16[512,4096]{1,0:T(8,128)(2,1)}, bf16[512,4096]{1,0:T(8,128)(2,1)})) %all-reduce.3.cloned.1.call-update) | async-done | bytes 8388624 | tf_op jit(solution)/shard_map/psum | solution.py:95
  475.6 13.6 %multiply_bitcast_fusion = (f32[64,32,8,128]{3,2,1,0:T(8,128)}, f32[64,32,8,128]{3,2,1,0:T(8,128)S(1)}) fusion(bf16[512,4096]{1,0:T(8,128)(2,1)} %get-tuple-element.7, f32[512,4096]{1,0:T(8,128)} %copy.19, f32[4096]{0:T(1024)S(1)} %add_convert_fusion, bf16[512,4096]{1,0:T(8,128)(2,1)} %get-tuple-element.6, f32[512,4096]{1,0:T(8,128)} %copy.13), kind=kLoop, calls=%fused_computation.22 | loop fusion | flops 16777216 | bytes 41959424
  489.2 13.2 %multiply_convert_fusion = bf16[512,32,128]{0,2,1:T(8,128)(2,1)} fusion(f32[64,32,8,128]{3,2,1,0:T(8,128)} %get-tuple-element.16), kind=kOutput, calls=%fused_computation.21 | convolution fusion | flops 3225812992 | bytes 12582912 | tf_op jit(solution)/shard_map/rbk,kj->rbj/dot_general | solution.py:30
  502.4 9.7 %multiply_convert_fusion.1 = bf16[512,32,128]{0,2,1:T(8,128)(2,1)} fusion(f32[64,32,8,128]{3,2,1,0:T(8,128)S(1)} %get-tuple-element.17), kind=kOutput, calls=%fused_computation.24 | convolution fusion | flops 3225812992 | bytes 12582912 | tf_op jit(solution)/shard_map/rbk,kj->rbj/dot_general | solution.py:30
  512.2 6.3 %copy.17 = bf16[512,4096]{1,0:T(8,128)(2,1)} copy(bf16[512,4096]{0,1:T(8,128)(2,1)} %bitcast.296) | data formatting | bytes 8388608 | tf_op jit(solution)/shard_map/convert_element_type | solution.py:96
  518.5 3.0 collective-permute-start
  521.5 6.3 %copy.24 = bf16[512,4096]{1,0:T(8,128)(2,1)} copy(bf16[512,4096]{0,1:T(8,128)(2,1)} %bitcast.295) | data formatting | bytes 8388608 | tf_op jit(solution)/shard_map/convert_element_type | solution.py:99
  527.8 0.0 collective-permute-start.1
  527.8 74.7 %collective-permute-done = bf16[512,4096]{1,0:T(8,128)(2,1)} collective-permute-done((bf16[512,4096]{1,0:T(8,128)(2,1)}, bf16[512,4096]{1,0:T(8,128)(2,1)}, u32[]{:S(2)}, u32[]{:S(2)}) %collective-permute-start) | collective-permute-done | bytes 4194336 | tf_op jit(solution)/shard_map/ppermute | solution.py:15
  602.5 11.5 %collective-permute-done.1 = bf16[512,4096]{1,0:T(8,128)(2,1)S(1)} collective-permute-done((bf16[512,4096]{1,0:T(8,128)(2,1)}, bf16[512,4096]{1,0:T(8,128)(2,1)S(1)}, u32[]{:S(2)}, u32[]{:S(2)}) %collective-permute-start.1) | collective-permute-done | bytes 4194336 | tf_op jit(solution)/shard_map/ppermute | solution.py:15
  614.0 4.8 copy.62
  618.9 2.0 copy.63
  (26 shorter events, 0.1 us)
Async XLA Ops:
  7.2 8.6 %copy-start = (bf16[1,2,4096,128]{3,2,1,0:T(8,128)(2,1)S(1)}, bf16[1,2,4096,128]{3,2,1,0:T(8,128)(2,1)}, u32[]{:S(2)}) copy-start(bf16[1,2,4096,128]{3,2,1,0:T(8,128)(2,1)} %param.17) | copy-start | bytes 6291460
  7.2 7.2 %copy-start.9 = (s32[4096]{0:T(1024)S(1)}, s32[4096]{0:T(1024)}, u32[]{:S(2)}) copy-start(s32[4096]{0:T(1024)} %param.14) | copy-start | bytes 49156
  7.2 8.5 %copy-start.10 = (f32[1,2,4096]{2,1,0:T(2,128)S(1)}, f32[1,2,4096]{2,1,0:T(2,128)}, u32[]{:S(2)}) copy-start(f32[1,2,4096]{2,1,0:T(2,128)} %param.15) | copy-start | bytes 98308
  7.2 468.4 %all-reduce.3.cloned.1.call-start = ((), (), s32[]{:S(2)}) async-start(), calls=%async_computation | async-start | bytes 16777216 | tf_op jit(solution)/shard_map/psum | solution.py:95
  15.8 3.7 copy-start.4
  19.5 4.9 copy-start.5
  24.4 2.2 copy-start.6
  27.9 12.1 %slice-start.2 = ((s8[8388608]{0:T(1024)(128)(4,1)}), s8[4194304]{0:T(1024)(128)(4,1)S(1)}, s32[]{:S(2)}) async-start(s8[8388608]{0:T(1024)(128)(4,1)} %bitcast.315), calls=%async_computation.3 | async-start | bytes 8388608
  35.7 4.2 slice-start.3
  39.9 3.2 copy-start.7
  44.0 2.0 copy-start.2
  46.0 11.1 %slice-start = ((s8[8388608]{0:T(1024)(128)(4,1)}), s8[4194304]{0:T(1024)(128)(4,1)S(1)}, s32[]{:S(2)}) async-start(s8[8388608]{0:T(1024)(128)(4,1)} %bitcast.313), calls=%async_computation.1 | async-start | bytes 8388608
  47.0 10.2 %slice-start.1 = ((s8[8388608]{0:T(1024)(128)(4,1)}), s8[4194304]{0:T(1024)(128)(4,1)S(1)}, s32[]{:S(2)}) async-start(s8[8388608]{0:T(1024)(128)(4,1)} %bitcast.313), calls=%async_computation.2 | async-start | bytes 8388608
  76.0 5.4 copy-start.3
  76.0 5.9 copy-start.8
  76.0 6.1 copy-start.14
  100.7 6.6 %copy-start.13 = (bf16[512,4,128]{0,2,1:T(8,128)(2,1)S(1)}, bf16[512,4,128]{0,2,1:T(8,128)(2,1)}, u32[]{:S(2)}) copy-start(bf16[512,4,128]{0,2,1:T(8,128)(2,1)} %fusion.74) | copy-start | bytes 1572868
  107.3 6.8 %copy-start.11 = (bf16[1,2,4096,128]{3,2,1,0:T(8,128)(2,1)S(1)}, bf16[1,2,4096,128]{3,2,1,0:T(8,128)(2,1)}, u32[]{:S(2)}) copy-start(bf16[1,2,4096,128]{3,2,1,0:T(8,128)(2,1)} %param.18) | copy-start | bytes 6291460
  107.3 6.8 %copy-start.12 = (bf16[512,512]{0,1:T(8,128)(2,1)S(1)}, bf16[512,512]{0,1:T(8,128)(2,1)}, u32[]{:S(2)}) copy-start(bf16[512,512]{0,1:T(8,128)(2,1)} %fusion.68) | copy-start | bytes 1572868
  518.5 84.1 %collective-permute-start = (bf16[512,4096]{1,0:T(8,128)(2,1)}, bf16[512,4096]{1,0:T(8,128)(2,1)}, u32[]{:S(2)}, u32[]{:S(2)}) collective-permute-start(bf16[512,4096]{1,0:T(8,128)(2,1)} %copy.17), channel_id=1, source_target_pairs={{0,8},{8,16},{16,24},{24,32},{32,40},{40,48},{48,56},{56,64},{64,7... | collective-permute-start | bytes 12582920 | tf_op jit(solution)/shard_map/ppermute | solution.py:15
  527.8 86.2 %collective-permute-start.1 = (bf16[512,4096]{1,0:T(8,128)(2,1)}, bf16[512,4096]{1,0:T(8,128)(2,1)S(1)}, u32[]{:S(2)}, u32[]{:S(2)}) collective-permute-start(bf16[512,4096]{1,0:T(8,128)(2,1)} %copy.24), channel_id=1, source_target_pairs={{0,120},{8,0},{16,8},{24,16},{32,24},{40,32},{48,40},{56,48},{64,5... | collective-permute-start | bytes 12582920 | tf_op jit(solution)/shard_map/ppermute | solution.py:15
  614.0 6.9 %copy-start.1 = (bf16[1,2,4096,128]{3,2,1,0:T(8,128)(2,1)S(1)}, bf16[1,2,4096,128]{3,2,1,0:T(8,128)(2,1)}, u32[]{:S(2)}) copy-start(bf16[1,2,4096,128]{3,2,1,0:T(8,128)(2,1)} %param.17) | copy-start | bytes 6291460
Sparse Core Ops, SparseCore 0:
  132.1 343.3 all-reduce.2
where the time goes:
time: 638 us; the launch traced here: 628 us
  waiting for transfers between devices  404 us (63%)
  matrix products  116 us (18%)
  local copies, waits for them, and re-layouts  45.1 us (7%)
  other arithmetic  41.7 us (7%)
  between operations  18.7 us (3%)
    psum x1, waiting for transfers between devices, local(): lax.psum(partial_out.astype(jnp.bfloat16), 'tensor').astype(jnp.float32)  317 us
    ppermute x2, waiting for transfers between devices, shifted(): return lax.ppermute(value, axis, pairs)  86.2 us
    dot_general x2, matrix products, rotate(): jnp.einsum('rbk,kj->rbj', blocks, hadamard(HB), precision=lax.Precision.H...  23 us
    dot_general x2, matrix products, unrotate(): jnp.einsum('rbk,kj->rbj', blocks, hadamard(HB), precision=lax.Precision.H...  18 us
    reshape x2, local copies, waits for them, and re-layouts, unrotate(): return (turned / math.sqrt(HB)).reshape(count, -1) * signs  17.9 us
    dot_general x3, matrix products, heads_part(): jnp.dot(normed, query_w, preferred_element_type=jnp.float32)  14.9 us
    unnamed x3, other arithmetic  13.6 us
    dot_general x3, matrix products, heads_part(): scores = jnp.einsum('qkgd,skd->kgqs', query, keys) / math.sqrt(HD)  13.1 us
  transfers between devices with their start and end apart: 3, of which 3 were waited for; matrix products, arithmetic and copies ran while one was open for 5% of the time, Pallas kernels for 0%

commit v1 on v0

--- a/solution.py
+++ b/solution.py
@@ -7,6 +7,10 @@
 HD = 128
 HB = 128
 eps = 1e-05
+
+
+def balance_shifts_all_now(work_x):
+    return lax.all_gather(work_x, "tensor").sum(axis=0)
 
 
 def shifted(value, axis, steps):
@@ -92,7 +96,7 @@
     partial_out = heads_part(inputs, gain_front, *front_w)
     _, pull = jax.vjp(lambda v: heads_part(v, gain_back, *back_w), stored)
     partial_back = pull(grad)[0]
-    mixed = lax.psum(partial_out.astype(jnp.bfloat16), "tensor").astype(jnp.float32)
+    mixed = balance_shifts_all_now(partial_out.astype(jnp.bfloat16)).astype(jnp.float32)
     sent_activation = rotate(inputs + mixed, signs).astype(jnp.bfloat16)
     arrived = shifted(sent_activation, "pipe", 1)
     pulled = lax.psum(partial_back.astype(jnp.bfloat16), "tensor").astype(jnp.float32)

time: 638 us -> 1110 us (1.74)
  waiting for transfers between devices: 404 us -> 867 us
    all_gather x0 -> x1, waiting for transfers between devices: none -> 664 us  [balance_shifts_all_now(): return lax.all_gather(work_x, 'tensor').sum(axis=0)]
    psum x1, waiting for transfers between devices: 317 us -> 157 us  [local(): lax.psum(partial_back.astype(jnp.bfloat16), 'tensor').astype(jnp.float32)]
    ppermute x2, waiting for transfers between devices: 86.2 us -> 45.8 us  [shifted(): return lax.ppermute(value, axis, pairs)]
    reduce_sum x0 -> x1, other arithmetic: none -> 14.4 us  [balance_shifts_all_now(): return lax.all_gather(work_x, 'tensor').sum(axis=0)]
    unnamed x3 -> x1, other arithmetic: 13.6 us -> 0.01 us
  transfers between devices with their start and end apart: 3 -> 4, of which waited for: 3 -> 3; matrix products, arithmetic and copies ran while one was open for 5% -> 9% of each run, Pallas kernels for 0% -> 0%
where the time goes in v1:
time: 1110 us; the launch traced here: 1100 us
  waiting for transfers between devices  867 us (78%)
  matrix products  125 us (11%)
  local copies, waits for them, and re-layouts  46.1 us (4%)
  other arithmetic  40.2 us (4%)
  between operations  18.6 us (2%)
    all_gather x1, waiting for transfers between devices, balance_shifts_all_now(): return lax.all_gather(work_x, 'tensor').sum(axis=0)  664 us
    psum x1, waiting for transfers between devices, local(): lax.psum(partial_back.astype(jnp.bfloat16), 'tensor').astype(jnp.float32)  157 us
    ppermute x2, waiting for transfers between devices, shifted(): return lax.ppermute(value, axis, pairs)  45.8 us
    dot_general x2, matrix products, rotate(): jnp.einsum('rbk,kj->rbj', blocks, hadamard(HB), precision=lax.Precision.H...  30.1 us
  transfers between devices with their start and end apart: 4, of which 3 were waited for; matrix products, arithmetic and copies ran while one was open for 9% of the time, Pallas kernels for 0%

profile of v1, /device:TPU:1, one launch (start us, length us, event | category | flops | bytes accessed | tf_op | source)
XLA Modules:
  0.0 1101.0 jit_solution(4065461815899490227)
XLA Ops:
  7.2 0.0 copy-start
  7.2 0.0 copy-start.9
  7.2 0.0 all-reduce.2.cloned.1.call-start
  7.2 1.4 fusion.198
  11.2 0.1 iota_compare_fusion
  11.3 3.1 fusion.3
  15.7 0.0 copy-done.9
  15.8 0.0 copy-start.4
  15.8 6.1 fusion.73
  21.8 0.0 copy-done
  21.9 0.0 copy-done.4
  21.9 1.3 fusion.98
  23.2 0.0 copy-start.8
  23.2 0.0 copy-start.5
  23.2 0.9 fusion.51
  24.1 0.0 copy-start.3
  24.1 2.0 copy-done.3
  26.1 0.9 fusion.120
  27.0 0.0 copy-done.8
  27.1 0.0 copy-done.5
  27.1 0.0 copy-start.6
  27.1 1.3 copy.46
  28.4 0.9 copy-done.6
  29.3 1.3 copy.45
  30.5 9.9 bitcast_multiply_fusion
  40.4 7.4 multiply_reduce_fusion
  47.8 0.0 copy-start.2
  47.8 0.0 slice-start.1
  47.8 1.7 multiply_convert_fusion.2
  49.6 2.5 copy-done.2
  52.1 0.0 slice-done
  52.1 1.1 slice-done.1
  53.1 3.2 fusion.67
  56.4 5.3 fusion.70
  61.7 6.9 convolution_convert_fusion.4
  68.6 8.8 convert_reduce_fusion
  77.4 5.4 fusion.192
  82.8 9.2 convolution_convert_fusion
  92.1 5.6 fusion.76
  97.7 0.0 copy-start.10
  97.8 6.8 convolution_convert_fusion.2
  104.6 11.6 %fusion.4 = (f32[512]{0:T(512)S(1)}, bf16[512,4096]{1,0:T(8,128)(2,1)}) fusion(bf16[1,512,4096]{2,1,0:T(8,128)(2,1)} %param.11, f32[4096]{0:T(1024)S(1)} %bitcast.312, bf16[512,4096]{1,0:T(8,128)(2,1)} %convolution_convert_fusion.2, bf16[512,4096]{1,0:T(8,128)(2,1)} %convolution_convert_fusion, bf16[1,2,4096,128]{3,2,1,0:T(8,128)(2,1)S(1)} %copy-done.10, ...), kind=kOutput, calls=%fused_computation.7 | convolution fusion | flops 835780096 | bytes 22841348 | tf_op jit(solution)/shard_map/transpose(jvp())/dot_general | solution.py:54
  116.2 6.2 fusion.7
  122.4 0.0 all-reduce.2.cloned.1.call-update
  122.5 0.0 all-gather.3.cloned.1.call-start
  122.5 5.5 fusion.79
  128.0 6.6 convolution_convert_fusion.3
  134.6 0.0 all-gather.3.cloned.1.call-update
  134.6 8.3 bitcast_multiply_fusion.1
  142.9 9.0 copy.31
  151.9 156.7 %all-reduce.2.cloned.1.call-done = bf16[512,4096]{1,0:T(8,128)(2,1)} async-done(((bf16[512,4096]{1,0:T(8,128)(2,1)}), bf16[512,4096]{1,0:T(8,128)(2,1)}) %all-reduce.2.cloned.1.call-update) | async-done | bytes 4194320 | tf_op jit(solution)/shard_map/psum | solution.py:102
  308.6 15.8 %multiply_convert_fusion = bf16[512,32,128]{0,2,1:T(8,128)(2,1)} fusion(bf16[512,4096]{1,0:T(8,128)(2,1)} %all-reduce.2.cloned.1.call-done, f32[512,4096]{1,0:T(8,128)} %copy.31, f32[4096]{0:T(1024)S(1)} %get-tuple-element.12), kind=kOutput, calls=%fused_computation.17 | convolution fusion | flops 3234201600 | bytes 16793600 | tf_op jit(solution)/shard_map/rbk,kj->rbj/dot_general | solution.py:34
  324.4 6.4 copy.36
  330.8 0.8 collective-permute-start.1
  331.6 664.4 %all-gather.3.cloned.1.call-done = bf16[4096,4096]{1,0:T(8,128)(2,1)} async-done(((bf16[512,4096]{1,0:T(8,128)(2,1)}), bf16[4096,4096]{1,0:T(8,128)(2,1)}) %all-gather.3.cloned.1.call-update) | async-done | bytes 33554448 | tf_op jit(solution)/shard_map/all_gather | solution.py:13
  996.1 14.4 %reduce_sum.98 = bf16[512,4096]{1,0:T(8,128)(2,1)} reduce(bf16[8,512,4096]{2,1,0:T(8,128)(2,1)} %bitcast.294, bf16[]{:T(256)} %constant.85.clone.1), dimensions={0}, to_apply=%region_3.4 | reduce | flops 14680064 | bytes 37748736 | tf_op jit(solution)/shard_map/reduce_sum | solution.py:13
  1010.4 7.1 copy.27
  1017.5 14.3 %multiply_convert_fusion.1 = bf16[512,32,128]{0,2,1:T(8,128)(2,1)} fusion(f32[512,32,128]{0,2,1:T(8,128)} %bitcast.293, f32[128,512,32]{1,0,2:T(8,128)} %copy-done.2, f32[32,128]{1,0:T(8,128)S(1)} %get-tuple-element.13, f32[32,128]{1,0:T(8,128)S(1)} %broadcast_multiply_fusion), kind=kOutput, calls=%fused_computation.20 | convolution fusion | flops 3232104448 | bytes 21004288 | tf_op jit(solution)/shard_map/rbk,kj->rbj/dot_general | solution.py:34
  1031.8 6.3 copy.29
  1038.2 3.0 collective-permute-start
  1041.1 0.0 collective-permute-done.1
  1041.1 45.8 %collective-permute-done = bf16[512,4096]{1,0:T(8,128)(2,1)S(1)} collective-permute-done((bf16[512,4096]{1,0:T(8,128)(2,1)}, bf16[512,4096]{1,0:T(8,128)(2,1)S(1)}, u32[]{:S(2)}, u32[]{:S(2)}) %collective-permute-start) | collective-permute-done | bytes 4194336 | tf_op jit(solution)/shard_map/ppermute | solution.py:19
  1086.9 2.1 copy.67
  1089.0 4.7 copy.68
  (18 shorter events, 0.1 us)
Async XLA Ops:
  7.2 14.7 %copy-start = (bf16[1,2,4096,128]{3,2,1,0:T(8,128)(2,1)S(1)}, bf16[1,2,4096,128]{3,2,1,0:T(8,128)(2,1)}, u32[]{:S(2)}) copy-start(bf16[1,2,4096,128]{3,2,1,0:T(8,128)(2,1)} %param.17) | copy-start | bytes 6291460
  7.2 8.5 copy-start.9
  7.2 301.4 %all-reduce.2.cloned.1.call-start = ((), (), s32[]{:S(2)}) async-start(), calls=%async_computation | async-start | bytes 8388608 | tf_op jit(solution)/shard_map/psum | solution.py:102
  15.8 6.1 copy-start.4
  23.2 3.8 copy-start.8
  23.2 3.8 copy-start.5
  24.1 2.0 copy-start.3
  27.1 2.2 copy-start.6
  40.4 11.7 %slice-start = ((s8[8388608]{0:T(1024)(128)(4,1)}), s8[4194304]{0:T(1024)(128)(4,1)S(1)}, s32[]{:S(2)}) async-start(s8[8388608]{0:T(1024)(128)(4,1)} %bitcast.315), calls=%async_computation.2 | async-start | bytes 8388608
  47.8 4.3 copy-start.2
  47.8 5.3 slice-start.1
  52.1 4.3 copy-start.7
  97.7 6.8 copy-start.10
  97.7 6.8 copy-start.11
  122.5 873.6 %all-gather.3.cloned.1.call-start = ((), (), s32[]{:S(2)}) async-start(), calls=%async_computation.1 | async-start | bytes 37748736 | tf_op jit(solution)/shard_map/all_gather | solution.py:13
  330.8 710.3 %collective-permute-start.1 = (bf16[512,4096]{1,0:T(8,128)(2,1)}, bf16[512,4096]{1,0:T(8,128)(2,1)}, u32[]{:S(2)}, u32[]{:S(2)}) collective-permute-start(bf16[512,4096]{1,0:T(8,128)(2,1)} %copy.36), channel_id=1, source_target_pairs={{0,120},{8,0},{16,8},{24,16},{32,24},{40,32},{48,40},{56,48},{64,5... | collective-permute-start | bytes 12582920 | tf_op jit(solution)/shard_map/ppermute | solution.py:19
  1038.2 48.7 %collective-permute-start = (bf16[512,4096]{1,0:T(8,128)(2,1)}, bf16[512,4096]{1,0:T(8,128)(2,1)S(1)}, u32[]{:S(2)}, u32[]{:S(2)}) collective-permute-start(bf16[512,4096]{1,0:T(8,128)(2,1)} %copy.29), channel_id=1, source_target_pairs={{0,8},{8,16},{16,24},{24,32},{32,40},{40,48},{48,56},{56,64},{64,7... | collective-permute-start | bytes 12582920 | tf_op jit(solution)/shard_map/ppermute | solution.py:19
  1086.9 6.9 copy-start.1
Sparse Core Ops, SparseCore 0:
  122.6 185.9 all-reduce.1
  310.8 685.1 all-gather.2
